TPU v7x, 32 devices: a whole 2x2x4 slice. The times are simulated.
32 devices in a mesh: pole: 2 (over y), row: 4 (over z), col: 2 (over x), sub: 2 (over core).
Axes of the slice: x: 2, y: 2, z: 4, core: 2. Of those that a mesh axis runs over, the one named last changes fastest.
Arguments:
- ainv: bfloat16 [4, 256, 128, 128], P(('pole', 'col'), ('row', 'sub')), parts along dimension 0, may hold values from -6 to 6
- lfac: bfloat16 [192, 8, 128, 128], P(('pole', 'row', 'col'), 'sub'), parts along dimension 0, may hold values from -0.1875 to 0.1875
- anc: int32 [96, 8], P(('row', 'col')), may hold values from 0 to 15, as said below
- dinv: float32 [192, 128, 128], P(('pole', 'row', 'col', 'sub')), parts along dimension 0, may hold values from -6 to 6
Outputs:
- ancestor_inv: bfloat16 [192, 8, 128, 128], P(('pole', 'row', 'col'), 'sub'), parts along dimension 0
- diag_inv: float32 [192, 128, 128], P(('pole', 'row', 'col', 'sub')), parts along dimension 0
There are 2 independent parts, one for each index of `pole`. A program takes and returns all parts, laid end to end along the dimension named above; an argument that names none is the same for every part. Nothing has to cross between parts.
Inputs may be any that keep to these rules, and one draw needn't show every extreme that they name: `anc`: each row lists 8 different ancestor indices in ascending order; its last 4 entries are always the subtree's top separators 16 - 4 .. 15.
All inputs are finite; a program needn't handle non-finite values.
Results may differ from a plain program's by a relative error of at most 0.0055.
Values may be sent and summed in bfloat16 or wider, within the bound.
A program may use at most 64 MiB of HBM per device.

v0:
```python
import jax
import jax.numpy as jnp
from jax import lax
from jax.sharding import PartitionSpec as P

NANC = 16


def shards(ainv, lfac, anc, dinv):
    slots = lfac.shape[1]
    width = lfac.shape[2]
    total_slots = anc.shape[1]
    sub_index = lax.axis_index("sub")
    panels = lax.all_gather(lfac, "sub", axis=1, tiled=True)
    table = lax.all_gather(ainv, ("row", "sub"), axis=1, tiled=True)[0]
    mine = lax.dynamic_slice_in_dim(anc, sub_index * slots, slots, 1)

    def one_whole(args):
        ids_mine, ids_all, panel = args
        flat = ids_mine[:, None] * NANC + ids_all[None, :]
        blocks = table[flat.reshape(-1)].reshape(slots, total_slots, width, width)
        return -jnp.einsum("ijab,jbc->iac", blocks, panel, preferred_element_type=jnp.float32)

    summed = lax.map(one_whole, (mine, anc, panels))
    ancestor_inv = summed.astype(jnp.bfloat16)
    terms = jnp.einsum("siba,sibc->sac", lfac, ancestor_inv, preferred_element_type=jnp.float32)
    total = lax.psum_scatter(
        terms.astype(jnp.bfloat16), "sub", scatter_dimension=0, tiled=True
    ).astype(jnp.float32)
    diag_inv = dinv - total
    return (ancestor_inv, diag_inv)


def solution(mesh):
    return jax.shard_map(
        shards,
        mesh=mesh,
        in_specs=(
            P(("pole", "col"), ("row", "sub"), None, None),
            P(("pole", "row", "col"), "sub", None, None),
            P(("row", "col"), None),
            P(("pole", "row", "col", "sub"), None, None),
        ),
        out_specs=(
            P(("pole", "row", "col"), "sub", None, None),
            P(("pole", "row", "col", "sub"), None, None),
        ),
        check_vma=False,
    )
```

profile of v0, /device:TPU:0, one launch (start us, length us, event | category | flops | bytes accessed | tf_op | source)
XLA Modules:
  0.0 203.7 jit_solution(12890412311361091690)
XLA Ops:
  8.0 0.7 all-gather.3.cloned.1.call-update
  8.9 15.5 %all-gather.5.cloned.1.call-done = bf16[12,8,128,128]{3,2,1,0:T(8,128)(2,1)} async-done(((bf16[12,4,128,128]{3,2,1,0:T(8,128)(2,1)}), bf16[12,8,128,128]{3,2,1,0:T(8,128)(2,1)}) %all-gather.5.cloned.1.call-update) | async-done | bytes 3145744 | tf_op jit(solution)/shard_map/all_gather | solution.py:14
  24.4 84.9 %all-gather.3.cloned.1.call-done = bf16[1,256,128,128]{3,2,0,1:T(8,128)(2,1)} async-done(((bf16[1,32,128,128]{3,2,0,1:T(8,128)(2,1)}), bf16[1,256,128,128]{3,2,0,1:T(8,128)(2,1)}) %all-gather.3.cloned.1.call-update) | async-done | bytes 8388624 | tf_op jit(solution)/shard_map/all_gather | solution.py:15
  109.3 76.7 %while.10 = (s32[]{:T(128)}, bf16[12,4,128,128]{3,2,1,0:T(8,128)(2,1)}, s32[12,4]{1,0:T(8,128)S(1)}, s32[12,8]{1,0:T(8,128)S(1)}, bf16[256,128,128]{2,1,0:T(8,12...) while((s32[]{:T(128)}, bf16[12,4,128,128]{3,2,1,0:T(8,128)(2,1)}, s32[12,4]{1,0:T(8,128)S(1)}, ...), condition=%wide.region_1.2_spmd, body=%wide.region_0.1_spmd.sunk | while | flops 134284416 | bytes 3676261 | solution.py:24
  109.5 4.2 %gather_fusion = bf16[32,128,128]{2,1,0:T(8,128)(2,1)S(1)} fusion(bf16[256,128,128]{2,1,0:T(8,128)(2,1)} %get-tuple-element.118, s32[1024]{0:T(1024)S(1)} %pad_clamp_fusion.2), kind=kCustom, calls=%fused_computation.clone.1 | custom fusion | bytes 2097280 | tf_op jit(solution)/shard_map/while/body/eval_jaxpr/gather | solution.py:21
  113.7 2.1 %fusion.26 = bf16[12,4,128,128]{3,2,1,0:T(8,128)(2,1)} fusion(bf16[12,4,128,128]{3,2,1,0:T(8,128)(2,1)} %get-tuple-element.108, s32[]{:T(128)} %get-tuple-element.107, bf16[4,8,128,128]{3,2,1,0:T(8,128)(2,1)S(1)} %bitcast.54, bf16[12,8,128,128]{3,2,1,0:T(8,128)(2,1)} %get-tuple-element.119), kind=kOutput, calls=%fused_computation.4.clone.1 | convolution fusion | flops 134283264 | bytes 1573888 | tf_op jit(solution)/shard_map/while/body/eval_jaxpr/ijab,jbc->iac/dot_general | solution.py:22
  115.9 4.1 %gather_fusion = bf16[32,128,128]{2,1,0:T(8,128)(2,1)S(1)} fusion(bf16[256,128,128]{2,1,0:T(8,128)(2,1)} %get-tuple-element.118, s32[1024]{0:T(1024)S(1)} %pad_clamp_fusion.2), kind=kCustom, calls=%fused_computation.clone.1 | custom fusion | bytes 2097280 | tf_op jit(solution)/shard_map/while/body/eval_jaxpr/gather | solution.py:21
  120.1 2.1 %fusion.26 = bf16[12,4,128,128]{3,2,1,0:T(8,128)(2,1)} fusion(bf16[12,4,128,128]{3,2,1,0:T(8,128)(2,1)} %get-tuple-element.108, s32[]{:T(128)} %get-tuple-element.107, bf16[4,8,128,128]{3,2,1,0:T(8,128)(2,1)S(1)} %bitcast.54, bf16[12,8,128,128]{3,2,1,0:T(8,128)(2,1)} %get-tuple-element.119), kind=kOutput, calls=%fused_computation.4.clone.1 | convolution fusion | flops 134283264 | bytes 1573888 | tf_op jit(solution)/shard_map/while/body/eval_jaxpr/ijab,jbc->iac/dot_general | solution.py:22
  122.3 4.1 %gather_fusion = bf16[32,128,128]{2,1,0:T(8,128)(2,1)S(1)} fusion(bf16[256,128,128]{2,1,0:T(8,128)(2,1)} %get-tuple-element.118, s32[1024]{0:T(1024)S(1)} %pad_clamp_fusion.2), kind=kCustom, calls=%fused_computation.clone.1 | custom fusion | bytes 2097280 | tf_op jit(solution)/shard_map/while/body/eval_jaxpr/gather | solution.py:21
  126.5 2.1 %fusion.26 = bf16[12,4,128,128]{3,2,1,0:T(8,128)(2,1)} fusion(bf16[12,4,128,128]{3,2,1,0:T(8,128)(2,1)} %get-tuple-element.108, s32[]{:T(128)} %get-tuple-element.107, bf16[4,8,128,128]{3,2,1,0:T(8,128)(2,1)S(1)} %bitcast.54, bf16[12,8,128,128]{3,2,1,0:T(8,128)(2,1)} %get-tuple-element.119), kind=kOutput, calls=%fused_computation.4.clone.1 | convolution fusion | flops 134283264 | bytes 1573888 | tf_op jit(solution)/shard_map/while/body/eval_jaxpr/ijab,jbc->iac/dot_general | solution.py:22
  128.7 4.1 %gather_fusion = bf16[32,128,128]{2,1,0:T(8,128)(2,1)S(1)} fusion(bf16[256,128,128]{2,1,0:T(8,128)(2,1)} %get-tuple-element.118, s32[1024]{0:T(1024)S(1)} %pad_clamp_fusion.2), kind=kCustom, calls=%fused_computation.clone.1 | custom fusion | bytes 2097280 | tf_op jit(solution)/shard_map/while/body/eval_jaxpr/gather | solution.py:21
  132.8 2.1 %fusion.26 = bf16[12,4,128,128]{3,2,1,0:T(8,128)(2,1)} fusion(bf16[12,4,128,128]{3,2,1,0:T(8,128)(2,1)} %get-tuple-element.108, s32[]{:T(128)} %get-tuple-element.107, bf16[4,8,128,128]{3,2,1,0:T(8,128)(2,1)S(1)} %bitcast.54, bf16[12,8,128,128]{3,2,1,0:T(8,128)(2,1)} %get-tuple-element.119), kind=kOutput, calls=%fused_computation.4.clone.1 | convolution fusion | flops 134283264 | bytes 1573888 | tf_op jit(solution)/shard_map/while/body/eval_jaxpr/ijab,jbc->iac/dot_general | solution.py:22
  135.1 4.1 %gather_fusion = bf16[32,128,128]{2,1,0:T(8,128)(2,1)S(1)} fusion(bf16[256,128,128]{2,1,0:T(8,128)(2,1)} %get-tuple-element.118, s32[1024]{0:T(1024)S(1)} %pad_clamp_fusion.2), kind=kCustom, calls=%fused_computation.clone.1 | custom fusion | bytes 2097280 | tf_op jit(solution)/shard_map/while/body/eval_jaxpr/gather | solution.py:21
  139.2 2.1 %fusion.26 = bf16[12,4,128,128]{3,2,1,0:T(8,128)(2,1)} fusion(bf16[12,4,128,128]{3,2,1,0:T(8,128)(2,1)} %get-tuple-element.108, s32[]{:T(128)} %get-tuple-element.107, bf16[4,8,128,128]{3,2,1,0:T(8,128)(2,1)S(1)} %bitcast.54, bf16[12,8,128,128]{3,2,1,0:T(8,128)(2,1)} %get-tuple-element.119), kind=kOutput, calls=%fused_computation.4.clone.1 | convolution fusion | flops 134283264 | bytes 1573888 | tf_op jit(solution)/shard_map/while/body/eval_jaxpr/ijab,jbc->iac/dot_general | solution.py:22
  141.5 4.1 %gather_fusion = bf16[32,128,128]{2,1,0:T(8,128)(2,1)S(1)} fusion(bf16[256,128,128]{2,1,0:T(8,128)(2,1)} %get-tuple-element.118, s32[1024]{0:T(1024)S(1)} %pad_clamp_fusion.2), kind=kCustom, calls=%fused_computation.clone.1 | custom fusion | bytes 2097280 | tf_op jit(solution)/shard_map/while/body/eval_jaxpr/gather | solution.py:21
  145.6 2.1 %fusion.26 = bf16[12,4,128,128]{3,2,1,0:T(8,128)(2,1)} fusion(bf16[12,4,128,128]{3,2,1,0:T(8,128)(2,1)} %get-tuple-element.108, s32[]{:T(128)} %get-tuple-element.107, bf16[4,8,128,128]{3,2,1,0:T(8,128)(2,1)S(1)} %bitcast.54, bf16[12,8,128,128]{3,2,1,0:T(8,128)(2,1)} %get-tuple-element.119), kind=kOutput, calls=%fused_computation.4.clone.1 | convolution fusion | flops 134283264 | bytes 1573888 | tf_op jit(solution)/shard_map/while/body/eval_jaxpr/ijab,jbc->iac/dot_general | solution.py:22
  147.8 4.1 %gather_fusion = bf16[32,128,128]{2,1,0:T(8,128)(2,1)S(1)} fusion(bf16[256,128,128]{2,1,0:T(8,128)(2,1)} %get-tuple-element.118, s32[1024]{0:T(1024)S(1)} %pad_clamp_fusion.2), kind=kCustom, calls=%fused_computation.clone.1 | custom fusion | bytes 2097280 | tf_op jit(solution)/shard_map/while/body/eval_jaxpr/gather | solution.py:21
  152.0 2.1 %fusion.26 = bf16[12,4,128,128]{3,2,1,0:T(8,128)(2,1)} fusion(bf16[12,4,128,128]{3,2,1,0:T(8,128)(2,1)} %get-tuple-element.108, s32[]{:T(128)} %get-tuple-element.107, bf16[4,8,128,128]{3,2,1,0:T(8,128)(2,1)S(1)} %bitcast.54, bf16[12,8,128,128]{3,2,1,0:T(8,128)(2,1)} %get-tuple-element.119), kind=kOutput, calls=%fused_computation.4.clone.1 | convolution fusion | flops 134283264 | bytes 1573888 | tf_op jit(solution)/shard_map/while/body/eval_jaxpr/ijab,jbc->iac/dot_general | solution.py:22
  154.2 4.1 %gather_fusion = bf16[32,128,128]{2,1,0:T(8,128)(2,1)S(1)} fusion(bf16[256,128,128]{2,1,0:T(8,128)(2,1)} %get-tuple-element.118, s32[1024]{0:T(1024)S(1)} %pad_clamp_fusion.2), kind=kCustom, calls=%fused_computation.clone.1 | custom fusion | bytes 2097280 | tf_op jit(solution)/shard_map/while/body/eval_jaxpr/gather | solution.py:21
  158.4 2.1 %fusion.26 = bf16[12,4,128,128]{3,2,1,0:T(8,128)(2,1)} fusion(bf16[12,4,128,128]{3,2,1,0:T(8,128)(2,1)} %get-tuple-element.108, s32[]{:T(128)} %get-tuple-element.107, bf16[4,8,128,128]{3,2,1,0:T(8,128)(2,1)S(1)} %bitcast.54, bf16[12,8,128,128]{3,2,1,0:T(8,128)(2,1)} %get-tuple-element.119), kind=kOutput, calls=%fused_computation.4.clone.1 | convolution fusion | flops 134283264 | bytes 1573888 | tf_op jit(solution)/shard_map/while/body/eval_jaxpr/ijab,jbc->iac/dot_general | solution.py:22
  160.6 4.1 %gather_fusion = bf16[32,128,128]{2,1,0:T(8,128)(2,1)S(1)} fusion(bf16[256,128,128]{2,1,0:T(8,128)(2,1)} %get-tuple-element.118, s32[1024]{0:T(1024)S(1)} %pad_clamp_fusion.2), kind=kCustom, calls=%fused_computation.clone.1 | custom fusion | bytes 2097280 | tf_op jit(solution)/shard_map/while/body/eval_jaxpr/gather | solution.py:21
  164.7 2.1 %fusion.26 = bf16[12,4,128,128]{3,2,1,0:T(8,128)(2,1)} fusion(bf16[12,4,128,128]{3,2,1,0:T(8,128)(2,1)} %get-tuple-element.108, s32[]{:T(128)} %get-tuple-element.107, bf16[4,8,128,128]{3,2,1,0:T(8,128)(2,1)S(1)} %bitcast.54, bf16[12,8,128,128]{3,2,1,0:T(8,128)(2,1)} %get-tuple-element.119), kind=kOutput, calls=%fused_computation.4.clone.1 | convolution fusion | flops 134283264 | bytes 1573888 | tf_op jit(solution)/shard_map/while/body/eval_jaxpr/ijab,jbc->iac/dot_general | solution.py:22
  167.0 4.1 %gather_fusion = bf16[32,128,128]{2,1,0:T(8,128)(2,1)S(1)} fusion(bf16[256,128,128]{2,1,0:T(8,128)(2,1)} %get-tuple-element.118, s32[1024]{0:T(1024)S(1)} %pad_clamp_fusion.2), kind=kCustom, calls=%fused_computation.clone.1 | custom fusion | bytes 2097280 | tf_op jit(solution)/shard_map/while/body/eval_jaxpr/gather | solution.py:21
  171.1 2.1 %fusion.26 = bf16[12,4,128,128]{3,2,1,0:T(8,128)(2,1)} fusion(bf16[12,4,128,128]{3,2,1,0:T(8,128)(2,1)} %get-tuple-element.108, s32[]{:T(128)} %get-tuple-element.107, bf16[4,8,128,128]{3,2,1,0:T(8,128)(2,1)S(1)} %bitcast.54, bf16[12,8,128,128]{3,2,1,0:T(8,128)(2,1)} %get-tuple-element.119), kind=kOutput, calls=%fused_computation.4.clone.1 | convolution fusion | flops 134283264 | bytes 1573888 | tf_op jit(solution)/shard_map/while/body/eval_jaxpr/ijab,jbc->iac/dot_general | solution.py:22
  173.4 4.1 %gather_fusion = bf16[32,128,128]{2,1,0:T(8,128)(2,1)S(1)} fusion(bf16[256,128,128]{2,1,0:T(8,128)(2,1)} %get-tuple-element.118, s32[1024]{0:T(1024)S(1)} %pad_clamp_fusion.2), kind=kCustom, calls=%fused_computation.clone.1 | custom fusion | bytes 2097280 | tf_op jit(solution)/shard_map/while/body/eval_jaxpr/gather | solution.py:21
  177.5 2.1 %fusion.26 = bf16[12,4,128,128]{3,2,1,0:T(8,128)(2,1)} fusion(bf16[12,4,128,128]{3,2,1,0:T(8,128)(2,1)} %get-tuple-element.108, s32[]{:T(128)} %get-tuple-element.107, bf16[4,8,128,128]{3,2,1,0:T(8,128)(2,1)S(1)} %bitcast.54, bf16[12,8,128,128]{3,2,1,0:T(8,128)(2,1)} %get-tuple-element.119), kind=kOutput, calls=%fused_computation.4.clone.1 | convolution fusion | flops 134283264 | bytes 1573888 | tf_op jit(solution)/shard_map/while/body/eval_jaxpr/ijab,jbc->iac/dot_general | solution.py:22
  179.7 4.1 %gather_fusion = bf16[32,128,128]{2,1,0:T(8,128)(2,1)S(1)} fusion(bf16[256,128,128]{2,1,0:T(8,128)(2,1)} %get-tuple-element.118, s32[1024]{0:T(1024)S(1)} %pad_clamp_fusion.2), kind=kCustom, calls=%fused_computation.clone.1 | custom fusion | bytes 2097280 | tf_op jit(solution)/shard_map/while/body/eval_jaxpr/gather | solution.py:21
  183.9 2.1 %fusion.26 = bf16[12,4,128,128]{3,2,1,0:T(8,128)(2,1)} fusion(bf16[12,4,128,128]{3,2,1,0:T(8,128)(2,1)} %get-tuple-element.108, s32[]{:T(128)} %get-tuple-element.107, bf16[4,8,128,128]{3,2,1,0:T(8,128)(2,1)S(1)} %bitcast.54, bf16[12,8,128,128]{3,2,1,0:T(8,128)(2,1)} %get-tuple-element.119), kind=kOutput, calls=%fused_computation.4.clone.1 | convolution fusion | flops 134283264 | bytes 1573888 | tf_op jit(solution)/shard_map/while/body/eval_jaxpr/ijab,jbc->iac/dot_general | solution.py:22
  185.9 2.8 %fusion.11 = bf16[12,128,128]{1,2,0:T(8,128)(2,1)} fusion(bf16[12,4,128,128]{3,2,1,0:T(8,128)(2,1)} %get-tuple-element.34, bf16[12,4,128,128]{3,2,1,0:T(8,128)(2,1)S(1)} %copy-done), kind=kOutput, calls=%fused_computation.19 | convolution fusion | flops 201523200 | bytes 3538944 | tf_op jit(solution)/shard_map/siba,sibc->sac/dot_general | solution.py:26
  189.0 6.3 %reduce-scatter.2.cloned.1.call-done = bf16[6,128,128]{1,2,0:T(8,128)(2,1)} async-done(((bf16[12,128,128]{1,2,0:T(8,128)(2,1)}), bf16[6,128,128]{1,2,0:T(8,128)(2,1)}) %reduce-scatter.2.cloned.1.call-update) | async-done | bytes 196624 | tf_op jit(solution)/shard_map/reduce_scatter | solution.py:27
  195.3 1.0 convert_subtract_fusion
  196.2 0.9 copy.16
  (87 shorter events, 3.4 us)
Async XLA Ops:
  7.2 1.6 copy-start.2
  7.2 17.2 %all-gather.5.cloned.1.call-start = ((), (), s32[]{:S(2)}) async-start(), calls=%async_computation.2 | async-start | bytes 4718592 | tf_op jit(solution)/shard_map/all_gather | solution.py:14
  7.9 101.4 %all-gather.3.cloned.1.call-start = ((), (), s32[]{:S(2)}) async-start(), calls=%async_computation.1 | async-start | bytes 9437184 | tf_op jit(solution)/shard_map/all_gather | solution.py:15
  8.7 186.6 %reduce-scatter.2.cloned.1.call-start = ((), (), s32[]{:S(2)}) async-start(), calls=%async_computation.3 | async-start | bytes 589824 | tf_op jit(solution)/shard_map/reduce_scatter | solution.py:27
  109.3 76.7 %copy-start = (bf16[12,4,128,128]{3,2,1,0:T(8,128)(2,1)S(1)}, bf16[12,4,128,128]{3,2,1,0:T(8,128)(2,1)}, u32[]{:S(2)}) copy-start(bf16[12,4,128,128]{3,2,1,0:T(8,128)(2,1)} %param.7) | copy-start | bytes 4718596
  185.9 2.9 %copy-start.1 = (f32[6,128,128]{2,1,0:T(8,128)S(1)}, f32[6,128,128]{2,1,0:T(8,128)}, u32[]{:S(2)}) copy-start(f32[6,128,128]{2,1,0:T(8,128)} %param.9) | copy-start | bytes 1179652
Sparse Core Ops, SparseCore 0:
  9.6 14.8 all-gather.4
  26.0 83.2 all-gather.2
  188.9 6.3 reduce-scatter.1
where the time goes:
time: 205 us; the launch traced here: 204 us
  waiting for transfers between devices  108 us (53%)
  local copies, waits for them, and re-layouts  52 us (25%)
  matrix products  27.4 us (13%)
  between operations  13.8 us (7%)
  other arithmetic  2.09 us (1%)
    all_gather x1, waiting for transfers between devices, shards(): table = lax.all_gather(ainv, ('row', 'sub'), axis=1, tiled=True)[0]  84.9 us
    gather x12, local copies, waits for them, and re-layouts, one_whole(): blocks = table[flat.reshape(-1)].reshape(slots, total_slots, width, width)  49.7 us
    dot_general x12, matrix products, one_whole(): jnp.einsum('ijab,jbc->iac', blocks, panel, preferred_element_type=jnp.flo...  24.6 us
    all_gather x1, waiting for transfers between devices, shards(): panels = lax.all_gather(lfac, 'sub', axis=1, tiled=True)  15.5 us
    reduce_scatter x1, waiting for transfers between devices, shards(): lax.psum_scatter(terms.astype(jnp.bfloat16), 'sub', scatter_dimension=0,...  6.29 us
  transfers between devices with their start and end apart: 3, of which 3 were waited for; matrix products, arithmetic and copies ran while one was open for 0% of the time, Pallas kernels for 0%

commit v1 on v0

v1 whole, which is shorter than its diff:
```python
import functools

import jax
import jax.numpy as jnp
from jax import lax
from jax.experimental import pallas as pl
from jax.experimental.pallas import tpu as pltpu
from jax.sharding import PartitionSpec as P

NANC = 16
MESH = pl.DeviceIdType.MESH


def kernel(
    chips, anc_ref, ainv_ref, lfac_ref, dinv_ref, inv_ref, diag_ref,
    table, panel, outgoing, incoming, kept, recv, send, psem, tsem,
):
    z = lax.axis_index("row")
    sub = lax.axis_index("sub")
    other = 1 - sub
    supers, slots, width, _ = lfac_ref.shape
    owned = ainv_ref.shape[1]
    half = supers // 2
    pieces = recv.shape[1]
    mine = pieces // 2
    size = owned // mine
    chunk_blocks = 2 * owned
    lower = table.shape[0] // chunk_blocks
    base = sub * (NANC - slots) * NANC

    def ours(chunk):
        return jnp.where(sub == 0, chunk < lower, chunk >= lower)

    def place(core, chunk, piece):
        return pl.ds((chunk - core * lower) * chunk_blocks + piece * size, size)

    def hop(chunk, piece, step):
        where = table.at[place(sub, chunk, piece)]
        return pltpu.make_async_remote_copy(
            src_ref=where,
            dst_ref=where,
            send_sem=send.at[0 if step > 0 else 1, chunk, piece],
            recv_sem=recv.at[chunk, piece],
            device_id={"row": z + step},
            device_id_type=MESH,
        )

    def own_local(q):
        return pltpu.make_async_copy(
            ainv_ref.at[0, pl.ds(q * size, size)],
            table.at[place(sub, z, sub * mine + q)],
            recv.at[z, sub * mine + q],
        )

    def own_across(q):
        return pltpu.make_async_remote_copy(
            src_ref=ainv_ref.at[0, pl.ds(q * size, size)],
            dst_ref=table.at[place(other, z, sub * mine + q)],
            send_sem=send.at[0, z, sub * mine + q],
            recv_sem=recv.at[z, sub * mine + q],
            device_id={"sub": other},
            device_id_type=MESH,
        )

    panel_local = pltpu.make_async_copy(lfac_ref, panel.at[sub], psem.at[0])
    panel_across = pltpu.make_async_remote_copy(
        src_ref=lfac_ref,
        dst_ref=panel.at[sub],
        send_sem=psem.at[1],
        recv_sem=psem.at[2],
        device_id={"sub": other},
        device_id_type=MESH,
    )
    terms_across = pltpu.make_async_remote_copy(
        src_ref=outgoing,
        dst_ref=incoming,
        send_sem=tsem.at[0],
        recv_sem=tsem.at[1],
        device_id={"sub": other},
        device_id_type=MESH,
    )

    at_home = ours(z)

    @pl.when(at_home)
    def _():
        for q in range(mine):
            own_local(q).start()

    panel_local.start()

    barrier = pltpu.get_barrier_semaphore()
    pl.semaphore_signal(barrier, inc=1, device_id={"sub": other}, device_id_type=MESH)

    @pl.when(z > 0)
    def _():
        pl.semaphore_signal(barrier, inc=1, device_id={"row": z - 1}, device_id_type=MESH)

    @pl.when(z < chips - 1)
    def _():
        pl.semaphore_signal(barrier, inc=1, device_id={"row": z + 1}, device_id_type=MESH)

    pl.semaphore_wait(barrier, 1 + jnp.where(z > 0, 1, 0) + jnp.where(z < chips - 1, 1, 0))

    @pl.when(jnp.logical_not(at_home))
    def _():
        for q in range(mine):
            own_across(q).start()

    def arrived(chunk, piece):
        where = table.at[place(sub, chunk, piece)]
        pltpu.make_async_copy(where, where, recv.at[chunk, piece]).wait()

    @pl.when(at_home)
    def _():
        @pl.loop(0, pieces)
        def _(piece):
            arrived(z, piece)

            @pl.when(z < chips - 1)
            def _():
                hop(z, piece, 1).start()

            @pl.when(z > 0)
            def _():
                hop(z, piece, -1).start()

    panel_across.start()

    @pl.loop(pieces, chips * pieces)
    def _(n):
        t = lax.div(n, pieces)
        piece = lax.rem(n, pieces)
        up = z - t
        down = z + t

        @pl.when(jnp.logical_and(up >= 0, ours(up)))
        def _():
            arrived(up, piece)

            @pl.when(z < chips - 1)
            def _():
                hop(up, piece, 1).start()

        @pl.when(jnp.logical_and(down < chips, ours(down)))
        def _():
            arrived(down, piece)

            @pl.when(z > 0)
            def _():
                hop(down, piece, -1).start()

    panel_local.wait()
    panel_across.wait()

    def work(s):
        ids = [anc_ref[s, j] for j in range(2 * slots)]
        rows = [jnp.maximum(anc_ref[s, sub * slots + i] * NANC - base, 0) for i in range(slots)]
        total = None
        for j in range(0, 2 * slots, 2):
            left = jnp.concatenate(
                [
                    jnp.concatenate([table[row + ids[j]], table[row + ids[j + 1]]], axis=1)
                    for row in rows
                ],
                axis=0,
            )
            right = panel[j // slots, s, pl.ds(j % slots, 2)].reshape(2 * width, width)
            part = jnp.dot(left, right, preferred_element_type=jnp.float32)
            total = part if total is None else total + part
        made = (-total).astype(jnp.bfloat16)
        inv_ref[s] = made.reshape(slots, width, width)
        return lax.dot_general(
            panel[sub, s].reshape(slots * width, width),
            made,
            (((0,), (0,)), ((), ())),
            preferred_element_type=jnp.float32,
        )

    @pl.loop(0, half)
    def _(n):
        outgoing[n] = work(n + other * half).astype(jnp.bfloat16)

    terms_across.start()

    @pl.loop(0, half)
    def _(n):
        kept[n] = work(n + sub * half)

    terms_across.wait()
    diag_ref[...] = dinv_ref[...] - (kept[...] + incoming[...].astype(jnp.float32))

    @pl.when(jnp.logical_not(at_home))
    def _():
        for q in range(mine):
            own_across(q).wait_send()

    @pl.loop(0, chips * pieces)
    def _(n):
        t = lax.div(n, pieces)
        piece = lax.rem(n, pieces)
        up = z - t
        down = z + t

        @pl.when(jnp.logical_and(jnp.logical_and(up >= 0, ours(up)), z < chips - 1))
        def _():
            hop(up, piece, 1).wait_send()

        @pl.when(jnp.logical_and(jnp.logical_and(down < chips, ours(down)), z > 0))
        def _():
            hop(down, piece, -1).wait_send()


def shards(chips, ainv, lfac, anc, dinv):
    supers, slots, width, _ = lfac.shape
    owned = ainv.shape[1]
    pieces = 2 * max(1, owned // 8)
    kept_rows = (NANC - slots) * NANC
    half = supers // 2
    vmem = pl.BlockSpec(memory_space=pltpu.VMEM)
    hbm = pl.BlockSpec(memory_space=pl.ANY)
    return pl.pallas_call(
        functools.partial(kernel, chips),
        out_shape=(
            jax.ShapeDtypeStruct(lfac.shape, jnp.bfloat16),
            jax.ShapeDtypeStruct(dinv.shape, jnp.float32),
        ),
        in_specs=[pl.BlockSpec(memory_space=pltpu.SMEM), hbm, hbm, vmem],
        out_specs=(vmem, vmem),
        scratch_shapes=[
            pltpu.VMEM((kept_rows, width, width), jnp.bfloat16),
            pltpu.VMEM((2, supers, slots, width, width), jnp.bfloat16),
            pltpu.VMEM((half, width, width), jnp.bfloat16),
            pltpu.VMEM((half, width, width), jnp.bfloat16),
            pltpu.VMEM((half, width, width), jnp.float32),
            pltpu.SemaphoreType.DMA((chips, pieces)),
            pltpu.SemaphoreType.DMA((2, chips, pieces)),
            pltpu.SemaphoreType.DMA((3,)),
            pltpu.SemaphoreType.DMA((2,)),
        ],
        compiler_params=pltpu.CompilerParams(
            collective_id=0, has_side_effects=True, vmem_limit_bytes=40 * 1024 * 1024
        ),
        cost_estimate=pl.CostEstimate(
            flops=2 * supers * slots * (2 * slots + 1) * width**3,
            bytes_accessed=2 * (kept_rows + 4 * supers * slots) * width**2,
            transcendentals=0,
        ),
    )(anc, ainv, lfac, dinv)


def solution(mesh):
    return jax.shard_map(
        functools.partial(shards, mesh.shape["row"]),
        mesh=mesh,
        in_specs=(
            P(("pole", "col"), ("row", "sub"), None, None),
            P(("pole", "row", "col"), "sub", None, None),
            P(("row", "col"), None),
            P(("pole", "row", "col", "sub"), None, None),
        ),
        out_specs=(
            P(("pole", "row", "col"), "sub", None, None),
            P(("pole", "row", "col", "sub"), None, None),
        ),
        check_vma=False,
    )
```

time: 205 us -> 90.9 us (0.44)
  waiting for transfers between devices: 108 us -> 0 us
  Pallas kernels: 0 us -> 83.7 us
  local copies, waits for them, and re-layouts: 52 us -> 6.29 us
  matrix products: 27.4 us -> 0 us
  between operations: 13.8 us -> 0.64 us
  other arithmetic: 2.09 us -> 0 us
    all_gather x2 -> x0, waiting for transfers between devices: 100 us -> none  [the longest x1 84.9 us: shards(): table = lax.all_gather(ainv, ('row', 'sub'), axis=1, tiled=True)[0]]
    pallas_call x0 -> x1, Pallas kernels: none -> 83.7 us  [shards(): pl.pallas_call(functools.partial(kernel, chips), out_shape=(jax.ShapeDtyp...]
    gather x12 -> x0, local copies, waits for them, and re-layouts: 49.7 us -> none  [one_whole(): blocks = table[flat.reshape(-1)].reshape(slots, total_slots, width, width)]
    dot_general x13 -> x0, matrix products: 27.4 us -> none  [the longest x12 24.6 us: one_whole(): jnp.einsum('ijab,jbc->iac', blocks, panel, preferred_element_type=jnp.flo...]
    reduce_scatter x1 -> x0, waiting for transfers between devices: 6.29 us -> none  [shards(): lax.psum_scatter(terms.astype(jnp.bfloat16), 'sub', scatter_dimension=0,...]
    unnamed x9, local copies, waits for them, and re-layouts: 1.17 us -> 6.29 us
  transfers between devices with their start and end apart: 3 -> 0, of which waited for: 3 -> 0; matrix products, arithmetic and copies ran while one was open for 0% -> 0% of each run, Pallas kernels for 0% -> 0%
where the time goes in v1:
time: 90.9 us; the launch traced here: 90.6 us
  Pallas kernels  83.7 us (92%)
  local copies, waits for them, and re-layouts  6.29 us (7%)
    pallas_call x1, Pallas kernels, shards(): pl.pallas_call(functools.partial(kernel, chips), out_shape=(jax.ShapeDtyp...  83.7 us
    unnamed x9, local copies, waits for them, and re-layouts  6.29 us

profile of v1, /device:TPU:0, one launch (start us, length us, event | category | flops | bytes accessed | tf_op | source)
XLA Modules:
  0.0 90.6 jit_solution(6364992271587043018)
XLA Ops:
  0.6 0.8 copy.6.anc_ref
  1.4 0.0 copy-start
  1.4 1.4 %copy-done = bf16[12,4,128,128]{3,2,1,0:T(8,128)(2,1)S(1)} copy-done((bf16[12,4,128,128]{3,2,1,0:T(8,128)(2,1)S(1)}, bf16[12,4,128,128]{3,2,1,0:T(8,128)(2,1)}, u32[]{:S(2)}) %copy-start) | copy-done | bytes 1572888
  2.8 0.0 copy-start.1
  2.8 1.2 %copy-done.1 = bf16[1,32,128,128]{3,2,1,0:T(8,128)(2,1)S(1)} copy-done((bf16[1,32,128,128]{3,2,1,0:T(8,128)(2,1)S(1)}, bf16[1,32,128,128]{3,2,1,0:T(8,128)(2,1)}, u32[]{:S(2)}) %copy-start.1) | copy-done | bytes 1048600
  4.0 0.0 copy-start.2
  4.0 1.0 %copy-done.2 = f32[6,128,128]{2,1,0:T(8,128)S(1)} copy-done((f32[6,128,128]{2,1,0:T(8,128)S(1)}, f32[6,128,128]{2,1,0:T(8,128)}, u32[]{:S(2)}) %copy-start.2) | copy-done | bytes 393240
  5.0 83.7 %shard_map.59 = (bf16[12,4,128,128]{3,2,1,0:T(8,128)(2,1)S(1)}, f32[6,128,128]{2,1,0:T(8,128)S(1)}) custom-call(s32[12,8]{1,0:T(8,128)S(1)} %copy.6.anc_ref, bf16[1,32,128,128]{3,2,1,0:T(8,128)(2,1)S(1)} %copy-done.1, bf16[12,4,128,128]{3,2,1,0:T(8,128)(2,1)S(1)} %copy-done, f32[6,128,128]{2,1,0:T(8,128)S(1)} %copy-done.2), custom_call_target="tpu_custom_call" | custom-call | flops 1811939328 | bytes 12582912 | tf_op jit(solution)/shard_map/pallas_call | solution.py:222
  88.7 1.1 %copy.9 = bf16[12,4,128,128]{3,2,1,0:T(8,128)(2,1)} copy(bf16[12,4,128,128]{3,2,1,0:T(8,128)(2,1)S(1)} %get-tuple-element.4) | data formatting | bytes 3145728
  89.9 0.7 copy.10
Async XLA Ops:
  1.4 1.4 %copy-start = (bf16[12,4,128,128]{3,2,1,0:T(8,128)(2,1)S(1)}, bf16[12,4,128,128]{3,2,1,0:T(8,128)(2,1)}, u32[]{:S(2)}) copy-start(bf16[12,4,128,128]{3,2,1,0:T(8,128)(2,1)} %lfac_ref.1) | copy-start | bytes 4718596
  2.8 1.2 %copy-start.1 = (bf16[1,32,128,128]{3,2,1,0:T(8,128)(2,1)S(1)}, bf16[1,32,128,128]{3,2,1,0:T(8,128)(2,1)}, u32[]{:S(2)}) copy-start(bf16[1,32,128,128]{3,2,1,0:T(8,128)(2,1)} %ainv_ref.1) | copy-start | bytes 3145732
  4.0 1.0 %copy-start.2 = (f32[6,128,128]{2,1,0:T(8,128)S(1)}, f32[6,128,128]{2,1,0:T(8,128)}, u32[]{:S(2)}) copy-start(f32[6,128,128]{2,1,0:T(8,128)} %dinv_ref.1) | copy-start | bytes 1179652

commit v2 on v1

v2 whole, which is shorter than its diff:
```python
import functools

import jax
import jax.numpy as jnp
from jax import lax
from jax.experimental import pallas as pl
from jax.experimental.pallas import tpu as pltpu
from jax.sharding import PartitionSpec as P

NANC = 16
MESH = pl.DeviceIdType.MESH


def kernel(
    chips, anc_ref, ainv_ref, lfac_ref, dinv_ref, inv_ref, diag_ref,
    tops, lows, panel, turned, partial, dinv, outgoing, incoming, kept,
    recv_top, recv_low, send_top, send_low, psem, tsem,
):
    z = lax.axis_index("row")
    sub = lax.axis_index("sub")
    other = 1 - sub
    supers, slots, width, _ = lfac_ref.shape
    half = supers // 2
    quarters = NANC // slots
    split = NANC - slots
    lower = chips * split // NANC
    base = sub * split
    owned_rows, held, _, _ = ainv_ref.shape
    whole = held == NANC
    top_count = 2
    low_count = 2 * owned_rows

    def valid(top, chunk, i):
        if whole:
            return True
        last = lax.rem(chunk * 2 + i, quarters) == quarters - 1
        return last if top else jnp.logical_not(last)

    def owner(top, i):
        return i if top else lax.div(i, owned_rows)

    def ours(chunk):
        return jnp.where(sub == 0, chunk < lower, chunk >= lower)

    def place(top, core, chunk, i):
        if whole:
            row = chunk * 2 * owned_rows - core * split
            if top:
                return tops.at[pl.ds(row + i * owned_rows, owned_rows)]
            return lows.at[pl.ds(row + i, 1)]
        quarter = chunk * 2 + i
        row = lax.div(quarter, quarters) - core * split
        if top:
            return tops.at[pl.ds(row, 1)]
        return lows.at[pl.ds(row, 1), pl.ds(lax.rem(quarter, quarters) * slots, slots)]

    def source(top, i):
        if not whole:
            return ainv_ref
        if top:
            return ainv_ref.at[:, pl.ds(split, slots)]
        return ainv_ref.at[pl.ds(i - sub * owned_rows, 1), pl.ds(0, split)]

    def arrival(top, chunk, i):
        return (recv_top if top else recv_low).at[chunk, i]

    def departure(top, step, chunk, i):
        return (send_top if top else send_low).at[0 if step > 0 else 1, chunk, i]

    def hop(top, chunk, i, step):
        where = place(top, sub, chunk, i)
        return pltpu.make_async_remote_copy(
            src_ref=where,
            dst_ref=where,
            send_sem=departure(top, step, chunk, i),
            recv_sem=arrival(top, chunk, i),
            device_id={"row": z + step},
            device_id_type=MESH,
        )

    def own_local(top, i):
        return pltpu.make_async_copy(
            source(top, i), place(top, sub, z, i), arrival(top, z, i)
        )

    def own_across(top, i):
        return pltpu.make_async_remote_copy(
            src_ref=source(top, i),
            dst_ref=place(top, other, z, i),
            send_sem=departure(top, 1, z, i),
            recv_sem=arrival(top, z, i),
            device_id={"sub": other},
            device_id_type=MESH,
        )

    panel_local = pltpu.make_async_copy(lfac_ref, panel.at[sub], psem.at[0])
    panel_across = pltpu.make_async_remote_copy(
        src_ref=lfac_ref,
        dst_ref=panel.at[sub],
        send_sem=psem.at[1],
        recv_sem=psem.at[2],
        device_id={"sub": other},
        device_id_type=MESH,
    )
    dinv_local = pltpu.make_async_copy(dinv_ref, dinv, psem.at[3])
    terms_across = pltpu.make_async_remote_copy(
        src_ref=outgoing,
        dst_ref=incoming,
        send_sem=tsem.at[0],
        recv_sem=tsem.at[1],
        device_id={"sub": other},
        device_id_type=MESH,
    )

    at_home = ours(z)

    def each_own(action):
        for top, count in ((True, top_count), (False, low_count)):
            @pl.loop(0, count)
            def _(i):
                @pl.when(jnp.logical_and(valid(top, z, i), owner(top, i) == sub))
                def _():
                    action(top, i)

    @pl.when(at_home)
    def _():
        each_own(lambda top, piece: own_local(top, piece).start())

    barrier = pltpu.get_barrier_semaphore()
    pl.semaphore_signal(barrier, inc=1, device_id={"sub": other}, device_id_type=MESH)

    @pl.when(z > 0)
    def _():
        pl.semaphore_signal(barrier, inc=1, device_id={"row": z - 1}, device_id_type=MESH)

    @pl.when(z < chips - 1)
    def _():
        pl.semaphore_signal(barrier, inc=1, device_id={"row": z + 1}, device_id_type=MESH)

    pl.semaphore_wait(barrier, 1 + jnp.where(z > 0, 1, 0) + jnp.where(z < chips - 1, 1, 0))

    @pl.when(jnp.logical_not(at_home))
    def _():
        each_own(lambda top, piece: own_across(top, piece).start())

    def arrived(top, chunk, i):
        where = place(top, sub, chunk, i)
        pltpu.make_async_copy(where, where, arrival(top, chunk, i)).wait()

    @pl.when(at_home)
    def _():
        for top, count in ((True, top_count), (False, low_count)):
            @pl.loop(0, count)
            def _(i):
                @pl.when(valid(top, z, i))
                def _():
                    arrived(top, z, i)

                    @pl.when(z < chips - 1)
                    def _():
                        hop(top, z, i, 1).start()

                    @pl.when(z > 0)
                    def _():
                        hop(top, z, i, -1).start()

    panel_local.start()
    panel_across.start()
    dinv_local.start()

    def relay(top, t, i):
        up = z - t
        down = z + t

        @pl.when(jnp.logical_and(jnp.logical_and(up >= 0, ours(up)), valid(top, up, i)))
        def _():
            arrived(top, up, i)

            @pl.when(z < chips - 1)
            def _():
                hop(top, up, i, 1).start()

        @pl.when(jnp.logical_and(jnp.logical_and(down < chips, ours(down)), valid(top, down, i)))
        def _():
            arrived(top, down, i)

            @pl.when(z > 0)
            def _():
                hop(top, down, i, -1).start()

    panel_local.wait()

    @pl.loop(0, supers)
    def _(s):
        turned[s] = panel[sub, s].reshape(slots * width, width).T

    panel_across.wait()

    def multiply(table, first, s):
        rows = [
            jnp.maximum(anc_ref[sub * slots + i, s] - base, 0) for i in range(slots)
        ]
        ids = [anc_ref[first * slots + j, s] for j in range(slots)]
        if first:
            ids = [jnp.maximum(b - (NANC - slots), 0) for b in ids]
        total = None
        for j in range(0, slots, 2):
            left = jnp.concatenate(
                [
                    jnp.concatenate([table[row, ids[j]], table[row, ids[j + 1]]], axis=1)
                    for row in rows
                ],
                axis=0,
            )
            right = panel[first, s, pl.ds(j, 2)].reshape(2 * width, width)
            part = jnp.dot(left, right, preferred_element_type=jnp.float32)
            total = part if total is None else total + part
        return total

    first_mine = sub * lower
    last_mine = jnp.where(sub == 0, lower, chips) - 1
    final = jnp.maximum(jnp.maximum(z - first_mine, last_mine - z), 1)
    share = -(-supers // low_count)

    @pl.loop(1, chips)
    def _(t):
        @pl.loop(0, top_count)
        def _(i):
            relay(True, t, i)

        @pl.loop(0, low_count)
        def _(i):
            @pl.when(t == final)
            def _():
                @pl.loop(0, share)
                def _(k):
                    s = i * share + k

                    @pl.when(s < supers)
                    def _():
                        partial[s] = multiply(tops, 1, s)

            relay(False, t, i)

    def work(s):
        made = (-(partial[s] + multiply(lows, 0, s))).astype(jnp.bfloat16)
        inv_ref[s] = made.reshape(slots, width, width)
        return jnp.dot(turned[s], made, preferred_element_type=jnp.float32)

    together = 2 if half % 2 == 0 else 1

    @pl.loop(0, half // together)
    def _(m):
        for u in range(together):
            n = m * together + u
            outgoing[n] = work(n + other * half).astype(jnp.bfloat16)

    terms_across.start()

    @pl.loop(0, half // together)
    def _(m):
        for u in range(together):
            n = m * together + u
            kept[n] = work(n + sub * half)

    dinv_local.wait()
    terms_across.wait()
    diag_ref[...] = dinv[...] - (kept[...] + incoming[...].astype(jnp.float32))

    @pl.when(jnp.logical_not(at_home))
    def _():
        each_own(lambda top, piece: own_across(top, piece).wait_send())

    @pl.loop(0, chips)
    def _(t):
        up = z - t
        down = z + t
        go_up = jnp.logical_and(jnp.logical_and(up >= 0, ours(up)), z < chips - 1)
        go_down = jnp.logical_and(jnp.logical_and(down < chips, ours(down)), z > 0)
        for top, count in ((True, top_count), (False, low_count)):
            @pl.loop(0, count)
            def _(i):
                @pl.when(jnp.logical_and(go_up, valid(top, up, i)))
                def _():
                    hop(top, up, i, 1).wait_send()

                @pl.when(jnp.logical_and(go_down, valid(top, down, i)))
                def _():
                    hop(top, down, i, -1).wait_send()


def shards(chips, ainv, lfac, anc, dinv):
    supers, slots, width, _ = lfac.shape
    owned = ainv.shape[1]
    held = min(owned, NANC)
    pieces = 2 * (owned // held)
    kept_rows = (NANC - slots) * NANC
    half = supers // 2
    vmem = pl.BlockSpec(memory_space=pltpu.VMEM)
    hbm = pl.BlockSpec(memory_space=pltpu.HBM)
    return pl.pallas_call(
        functools.partial(kernel, chips),
        out_shape=(
            pltpu.VMEM(lfac.shape, jnp.bfloat16),
            pltpu.VMEM(dinv.shape, jnp.float32),
        ),
        in_specs=[pl.BlockSpec(memory_space=pltpu.SMEM), hbm, hbm, hbm],
        out_specs=(vmem, vmem),
        scratch_shapes=[
            pltpu.VMEM((NANC - slots, slots, width, width), jnp.bfloat16),
            pltpu.VMEM((NANC - slots, NANC - slots, width, width), jnp.bfloat16),
            pltpu.VMEM((2, supers, slots, width, width), jnp.bfloat16),
            pltpu.VMEM((supers, width, slots * width), jnp.bfloat16),
            pltpu.VMEM((supers, slots * width, width), jnp.float32),
            pltpu.VMEM(dinv.shape, jnp.float32),
            pltpu.VMEM((half, width, width), jnp.bfloat16),
            pltpu.VMEM((half, width, width), jnp.bfloat16),
            pltpu.VMEM((half, width, width), jnp.float32),
            pltpu.SemaphoreType.DMA((chips, 2)),
            pltpu.SemaphoreType.DMA((chips, pieces)),
            pltpu.SemaphoreType.DMA((2, chips, 2)),
            pltpu.SemaphoreType.DMA((2, chips, pieces)),
            pltpu.SemaphoreType.DMA((4,)),
            pltpu.SemaphoreType.DMA((2,)),
        ],
        compiler_params=pltpu.CompilerParams(
            collective_id=0, has_side_effects=True, vmem_limit_bytes=60 * 1024 * 1024
        ),
        cost_estimate=pl.CostEstimate(
            flops=2 * supers * slots * (2 * slots + 1) * width**3,
            bytes_accessed=2 * (kept_rows + 4 * supers * slots) * width**2,
            transcendentals=0,
        ),
    )(anc.T, ainv.reshape(owned // held, held, width, width), lfac, dinv)


def solution(mesh):
    return jax.shard_map(
        functools.partial(shards, mesh.shape["row"]),
        mesh=mesh,
        in_specs=(
            P(("pole", "col"), ("row", "sub"), None, None),
            P(("pole", "row", "col"), "sub", None, None),
            P(("row", "col"), None),
            P(("pole", "row", "col", "sub"), None, None),
        ),
        out_specs=(
            P(("pole", "row", "col"), "sub", None, None),
            P(("pole", "row", "col", "sub"), None, None),
        ),
        check_vma=False,
    )
```

time: 90.9 us -> 82.6 us (0.909)
  local copies, waits for them, and re-layouts: 6.29 us -> 1.89 us
  Pallas kernels: 83.7 us -> 79.9 us
    unnamed x9 -> x2, local copies, waits for them, and re-layouts: 6.29 us -> 1.89 us
    pallas_call x1, Pallas kernels: 83.7 us -> 79.9 us  [shards(): pl.pallas_call(functools.partial(kernel, chips), out_shape=(pltpu.VMEM(lf...]
where the time goes in v2:
time: 82.6 us; the launch traced here: 82.4 us
  Pallas kernels  79.9 us (97%)
  local copies, waits for them, and re-layouts  1.89 us (2%)
    pallas_call x1, Pallas kernels, shards(): pl.pallas_call(functools.partial(kernel, chips), out_shape=(pltpu.VMEM(lf...  79.9 us
    unnamed x2, local copies, waits for them, and re-layouts  1.89 us

profile of v2, /device:TPU:0, one launch (start us, length us, event | category | flops | bytes accessed | tf_op | source)
XLA Modules:
  0.0 82.4 jit_solution(2013882017821822466)
XLA Ops:
  0.6 79.9 %shard_map.59 = (bf16[12,4,128,128]{3,2,1,0:T(8,128)(2,1)S(1)}, f32[6,128,128]{2,1,0:T(8,128)S(1)}) custom-call(s32[8,12]{1,0:T(8,128)} %bitcast.3, bf16[2,16,128,128]{3,2,1,0:T(8,128)(2,1)} %bitcast.2, bf16[12,4,128,128]{3,2,1,0:T(8,128)(2,1)} %lfac_ref.1, f32[6,128,128]{2,1,0:T(8,128)} %dinv_ref.1), custom_call_target="tpu_custom_call" | custom-call | flops 1811939328 | bytes 12582912 | tf_op jit(solution)/shard_map/pallas_call | solution.py:301
  80.6 1.1 %copy.8 = bf16[12,4,128,128]{3,2,1,0:T(8,128)(2,1)} copy(bf16[12,4,128,128]{3,2,1,0:T(8,128)(2,1)S(1)} %get-tuple-element.2) | data formatting | bytes 3145728
  81.7 0.7 copy.9

commit v3 on v2

--- a/solution.py
+++ b/solution.py
@@ -67,10 +67,10 @@
     def departure(top, step, chunk, i):
         return (send_top if top else send_low).at[0 if step > 0 else 1, chunk, i]
 
-    def hop(top, chunk, i, step):
+    def hop(top, chunk, i, step, origin=None):
         where = place(top, sub, chunk, i)
         return pltpu.make_async_remote_copy(
-            src_ref=where,
+            src_ref=where if origin is None else origin,
             dst_ref=where,
             send_sem=departure(top, step, chunk, i),
             recv_sem=arrival(top, chunk, i),
@@ -147,22 +147,28 @@
         where = place(top, sub, chunk, i)
         pltpu.make_async_copy(where, where, arrival(top, chunk, i)).wait()
 
+    def spread(top, i, origin):
+        @pl.when(z < chips - 1)
+        def _():
+            hop(top, z, i, 1, origin).start()
+
+        @pl.when(z > 0)
+        def _():
+            hop(top, z, i, -1, origin).start()
+
     @pl.when(at_home)
     def _():
+        each_own(lambda top, i: spread(top, i, source(top, i)))
+
         for top, count in ((True, top_count), (False, low_count)):
             @pl.loop(0, count)
             def _(i):
-                @pl.when(valid(top, z, i))
+                @pl.when(jnp.logical_and(valid(top, z, i), owner(top, i) != sub))
                 def _():
                     arrived(top, z, i)
-
-                    @pl.when(z < chips - 1)
-                    def _():
-                        hop(top, z, i, 1).start()
-
-                    @pl.when(z > 0)
-                    def _():
-                        hop(top, z, i, -1).start()
+                    spread(top, i, None)
+
+        each_own(lambda top, i: arrived(top, z, i))
 
     panel_local.start()
     panel_across.start()
@@ -247,7 +253,7 @@
         inv_ref[s] = made.reshape(slots, width, width)
         return jnp.dot(turned[s], made, preferred_element_type=jnp.float32)
 
-    together = 2 if half % 2 == 0 else 1
+    together = 3 if half % 3 == 0 else 1
 
     @pl.loop(0, half // together)
     def _(m):

time: 82.6 us -> 82 us (level)
  Pallas kernels: 79.9 us -> 79 us
    pallas_call x1, Pallas kernels: 79.9 us -> 79 us  [shards(): pl.pallas_call(functools.partial(kernel, chips), out_shape=(pltpu.VMEM(lf...]
where the time goes in v3:
time: 82 us; the launch traced here: 81.5 us
  Pallas kernels  79 us (96%)
  local copies, waits for them, and re-layouts  1.89 us (2%)
    pallas_call x1, Pallas kernels, shards(): pl.pallas_call(functools.partial(kernel, chips), out_shape=(pltpu.VMEM(lf...  79 us
    unnamed x2, local copies, waits for them, and re-layouts  1.89 us

profile of v3, /device:TPU:0, one launch (start us, length us, event | category | flops | bytes accessed | tf_op | source)
XLA Modules:
  0.0 81.5 jit_solution(4587930206087187791)
XLA Ops:
  0.6 79.0 %shard_map.59 = (bf16[12,4,128,128]{3,2,1,0:T(8,128)(2,1)S(1)}, f32[6,128,128]{2,1,0:T(8,128)S(1)}) custom-call(s32[8,12]{1,0:T(8,128)} %bitcast.3, bf16[2,16,128,128]{3,2,1,0:T(8,128)(2,1)} %bitcast.2, bf16[12,4,128,128]{3,2,1,0:T(8,128)(2,1)} %lfac_ref.1, f32[6,128,128]{2,1,0:T(8,128)} %dinv_ref.1), custom_call_target="tpu_custom_call" | custom-call | flops 1811939328 | bytes 12582912 | tf_op jit(solution)/shard_map/pallas_call | solution.py:307
  79.6 1.1 %copy.8 = bf16[12,4,128,128]{3,2,1,0:T(8,128)(2,1)} copy(bf16[12,4,128,128]{3,2,1,0:T(8,128)(2,1)S(1)} %get-tuple-element.2) | data formatting | bytes 3145728
  80.8 0.7 copy.9

commit v4 on v3

--- a/solution.py
+++ b/solution.py
@@ -28,7 +28,7 @@
     owned_rows, held, _, _ = ainv_ref.shape
     whole = held == NANC
     top_count = 2
-    low_count = 2 * owned_rows
+    low_count = 2
 
     def valid(top, chunk, i):
         if whole:
@@ -37,7 +37,7 @@
         return last if top else jnp.logical_not(last)
 
     def owner(top, i):
-        return i if top else lax.div(i, owned_rows)
+        return i
 
     def ours(chunk):
         return jnp.where(sub == 0, chunk < lower, chunk >= lower)
@@ -47,7 +47,7 @@
             row = chunk * 2 * owned_rows - core * split
             if top:
                 return tops.at[pl.ds(row + i * owned_rows, owned_rows)]
-            return lows.at[pl.ds(row + i, 1)]
+            return lows.at[pl.ds(row + i * owned_rows, owned_rows)]
         quarter = chunk * 2 + i
         row = lax.div(quarter, quarters) - core * split
         if top:
@@ -59,7 +59,7 @@
             return ainv_ref
         if top:
             return ainv_ref.at[:, pl.ds(split, slots)]
-        return ainv_ref.at[pl.ds(i - sub * owned_rows, 1), pl.ds(0, split)]
+        return ainv_ref.at[:, pl.ds(0, split)]
 
     def arrival(top, chunk, i):
         return (recv_top if top else recv_low).at[chunk, i]
@@ -253,7 +253,7 @@
         inv_ref[s] = made.reshape(slots, width, width)
         return jnp.dot(turned[s], made, preferred_element_type=jnp.float32)
 
-    together = 3 if half % 3 == 0 else 1
+    together = 6 if half % 6 == 0 else 1
 
     @pl.loop(0, half // together)
     def _(m):
@@ -299,7 +299,7 @@
     supers, slots, width, _ = lfac.shape
     owned = ainv.shape[1]
     held = min(owned, NANC)
-    pieces = 2 * (owned // held)
+    pieces = 2
     kept_rows = (NANC - slots) * NANC
     half = supers // 2
     vmem = pl.BlockSpec(memory_space=pltpu.VMEM)

time: 82 us -> 81.3 us (level)
  Pallas kernels: 79 us -> 78 us
    pallas_call x1, Pallas kernels: 79 us -> 78 us  [shards(): pl.pallas_call(functools.partial(kernel, chips), out_shape=(pltpu.VMEM(lf...]
where the time goes in v4:
time: 81.3 us; the launch traced here: 80.5 us
  Pallas kernels  78 us (96%)
  local copies, waits for them, and re-layouts  1.89 us (2%)
    pallas_call x1, Pallas kernels, shards(): pl.pallas_call(functools.partial(kernel, chips), out_shape=(pltpu.VMEM(lf...  78 us
    unnamed x2, local copies, waits for them, and re-layouts  1.89 us

profile of v4, /device:TPU:0, one launch (start us, length us, event | category | flops | bytes accessed | tf_op | source)
XLA Modules:
  0.0 80.5 jit_solution(10832876202012773137)
XLA Ops:
  0.6 78.0 %shard_map.59 = (bf16[12,4,128,128]{3,2,1,0:T(8,128)(2,1)S(1)}, f32[6,128,128]{2,1,0:T(8,128)S(1)}) custom-call(s32[8,12]{1,0:T(8,128)} %bitcast.3, bf16[2,16,128,128]{3,2,1,0:T(8,128)(2,1)} %bitcast.2, bf16[12,4,128,128]{3,2,1,0:T(8,128)(2,1)} %lfac_ref.1, f32[6,128,128]{2,1,0:T(8,128)} %dinv_ref.1), custom_call_target="tpu_custom_call" | custom-call | flops 1811939328 | bytes 12582912 | tf_op jit(solution)/shard_map/pallas_call | solution.py:307
  78.6 1.1 %copy.8 = bf16[12,4,128,128]{3,2,1,0:T(8,128)(2,1)} copy(bf16[12,4,128,128]{3,2,1,0:T(8,128)(2,1)S(1)} %get-tuple-element.2) | data formatting | bytes 3145728
  79.8 0.7 copy.9
